TPU v7x, 128 devices: a whole 4x4x4 slice. The times are simulated.
128 devices in a mesh: dp: 8 (over z, y_hi), tensor: 16 (over x, y_lo, core).
Axes of the slice: x: 4, y: 4 (y_hi: 2, y_lo: 2; y = y_hi * 2 + y_lo), z: 4, core: 2. Of those that a mesh axis runs over, the one named last changes fastest.
Arguments:
- hidden_train: bfloat16 [32, 1024, 28672], P('dp', None, 'tensor'), may hold values from -6 to 6
- outgrad_train: bfloat16 [32, 1024, 8192], P('dp', None, 'tensor'), may hold values from -6 to 6
- hidden_query: bfloat16 [8, 1024, 28672], P('dp', None, 'tensor'), may hold values from -6 to 6
- outgrad_query: bfloat16 [8, 1024, 8192], P('dp', None, 'tensor'), may hold values from -6 to 6
- proj_in: bfloat16 [28672, 64], P('tensor'), may hold values from -0.03125 to 0.03125
- proj_out: bfloat16 [8192, 64], P('tensor'), may hold values from -0.0625 to 0.0625
Outputs:
- train_grads: float32 [32, 4096], P('dp', 'tensor')
- scores: float32 [32, 8], P('dp')
All inputs are finite; a program needn't handle non-finite values.
Results may differ from a plain program's by a relative error of at most 0.0003.
Values sent between devices are 32-bit elements; how exact they have to be, the bound alone decides.
A program may use at most 128 MiB of HBM per device.

v0:
```python
import jax
import jax.numpy as jnp
from jax import lax
from jax.sharding import PartitionSpec as P


def partials(hidden, outgrad, proj_in, proj_out):
    count = hidden.shape[0] * hidden.shape[1]
    first = jnp.dot(
        hidden.reshape(count, hidden.shape[2]), proj_in, preferred_element_type=jnp.float32
    )
    second = jnp.dot(
        outgrad.reshape(count, outgrad.shape[2]), proj_out, preferred_element_type=jnp.float32
    )
    return jnp.concatenate([first, second], axis=1)


def outer_sums(stacked, length, rank):
    first = stacked[:, :, :rank]
    second = stacked[:, :, rank:]
    outer = jnp.einsum("str,stk->srk", first, second, precision=lax.Precision.HIGHEST)
    outer = outer / jnp.sqrt(jnp.float32(length))
    return outer.reshape(stacked.shape[0], rank * rank)


def on_device(hidden_train, outgrad_train, hidden_query, outgrad_query, proj_in, proj_out):
    train_count = hidden_train.shape[0]
    length = hidden_train.shape[1]
    rank = proj_in.shape[1]
    stacked = jnp.concatenate(
        [
            partials(hidden_train, outgrad_train, proj_in, proj_out),
            partials(hidden_query, outgrad_query, proj_in, proj_out),
        ],
        axis=0,
    )
    stacked = stacked.reshape(-1, length, 2 * rank)
    share = rank * rank // lax.axis_size("tensor")
    summed = lax.psum(stacked, "tensor")
    grads = outer_sums(summed, length, rank)
    train_full = grads[:train_count]
    every_query = lax.all_gather(grads[train_count:], "dp", axis=0, tiled=True)
    scores = jnp.dot(train_full, every_query.T, precision=lax.Precision.HIGHEST) / rank
    start = lax.axis_index("tensor") * share
    train_grads = lax.dynamic_slice_in_dim(train_full, start, share, 1)
    return (train_grads, scores)


def solution(mesh):
    placed = (
        P("dp", None, "tensor"),
        P("dp", None, "tensor"),
        P("dp", None, "tensor"),
        P("dp", None, "tensor"),
        P("tensor", None),
        P("tensor", None),
    )
    return jax.shard_map(
        on_device,
        mesh=mesh,
        in_specs=placed,
        out_specs=(P("dp", "tensor"), P("dp", None)),
        check_vma=False,
    )
```

profile of v0, /device:TPU:0, one launch (start us, length us, event | category | flops | bytes accessed | tf_op | source)
XLA Modules:
  0.0 205.0 jit_solution(16943059266049593662)
XLA Ops:
  7.2 0.0 copy-start
  7.2 0.0 all-reduce.2.cloned.1.call-start
  7.2 1.2 copy-done
  8.4 0.0 copy-start.1
  8.4 1.4 fusion.10
  9.8 3.9 %fusion.15 = f32[4096,64]{0,1:T(8,128)S(1)} fusion(bf16[4096,512]{1,0:T(8,128)(2,1)} %bitcast.21, bf16[512,64]{0,1:T(8,128)(2,1)} %param.11), kind=kOutput, calls=%fused_computation.14 | convolution fusion | flops 268435456 | bytes 5308416 | tf_op jit(solution)/shard_map/dot_general | solution.py:12
  13.8 3.4 %fusion = f32[1024,64]{0,1:T(8,128)S(1)} fusion(bf16[1792,64]{0,1:T(8,128)(2,1)} %param.10, bf16[1,1024,1792]{2,1,0:T(8,128)(2,1)} %param.8), kind=kOutput, calls=%fused_computation | convolution fusion | flops 234881024 | bytes 4161536 | tf_op jit(solution)/shard_map/dot_general | solution.py:9
  17.1 0.0 copy-done.1
  17.1 5.4 %fusion.14 = f32[4096,64]{0,1:T(8,128)S(1)} fusion(bf16[4096,1792]{1,0:T(8,128)(2,1)S(1)} %bitcast.19, bf16[1792,64]{0,1:T(8,128)(2,1)} %param.10), kind=kOutput, calls=%fused_computation.13 | convolution fusion | flops 939524096 | bytes 15958016 | tf_op jit(solution)/shard_map/dot_general | solution.py:9
  22.6 1.7 maximum_maximum_fusion
  24.3 3.2 %copy.11 = f32[5120,128]{1,0:T(8,128)} copy(f32[5120,128]{0,1:T(8,128)} %maximum_maximum_fusion) | data formatting | bytes 5242880 | tf_op jit(solution)/shard_map/concatenate | solution.py:30
  27.5 3.2 %copy.12 = f32[5,1024,128]{1,2,0:T(8,128)} copy(f32[5,1024,128]{2,1,0:T(8,128)} %bitcast.20) | data formatting | bytes 5242880 | tf_op jit(solution)/shard_map/reshape | solution.py:37
  30.7 0.0 all-reduce.2.cloned.1.call-update
  30.8 127.9 %all-reduce.2.cloned.1.call-done = f32[5,1024,128]{1,2,0:T(8,128)} async-done(((f32[5,1024,128]{1,2,0:T(8,128)}), f32[5,1024,128]{1,2,0:T(8,128)}) %all-reduce.2.cloned.1.call-update) | async-done | bytes 2621456 | tf_op jit(solution)/shard_map/psum | solution.py:39
  158.7 3.0 %fusion.5 = f32[5,64,64]{2,1,0:T(8,128)S(1)} fusion(f32[5,1024,128]{1,2,0:T(8,128)} %all-reduce.2.cloned.1.call-done), kind=kOutput, calls=%fused_computation.6 | convolution fusion | flops 251678720 | bytes 2703360 | tf_op jit(solution)/shard_map/str,stk->srk/dot_general | solution.py:21
  161.7 0.1 slice.21
  161.9 0.1 reshape.27
  161.9 34.6 %all-gather = f32[8,1,4096]{2,1,0:T(1,128)S(1)} all-gather(f32[1,1,4096]{2,1,0:T(1,128)S(1)} %reshape.27), channel_id=1, replica_groups=mesh['dp'=8,'tensor'=16] {'dp'}, dimensions={0}, use_global_device_ids=true | all-gather | bytes 147456 | tf_op jit(solution)/shard_map/all_gather | solution.py:42
  196.6 0.6 constant_dynamic-slice_fusion
  197.2 1.0 convolution_multiply_fusion
  (2 shorter events, 0.0 us)
Async XLA Ops:
  7.2 1.2 copy-start
  7.2 151.5 %all-reduce.2.cloned.1.call-start = ((), (), s32[]{:S(2)}) async-start(), calls=%async_computation | async-start | bytes 5242880 | tf_op jit(solution)/shard_map/psum | solution.py:39
  8.4 8.7 %copy-start.1 = (bf16[4,1024,1792]{2,1,0:T(8,128)(2,1)S(1)}, bf16[4,1024,1792]{2,1,0:T(8,128)(2,1)}, u32[]{:S(2)}) copy-start(bf16[4,1024,1792]{2,1,0:T(8,128)(2,1)} %param.6) | copy-start | bytes 44040196
Sparse Core Ops, SparseCore 0:
  30.9 127.7 all-reduce.1
where the time goes:
time: 205 us
  waiting for transfers between devices  128 us (62%)
  blocking collectives  34.6 us (17%)
  matrix products  18.2 us (9%)
  between operations  14.1 us (7%)
  local copies, waits for them, and re-layouts  8.44 us (4%)
    psum x1, waiting for transfers between devices, on_device(): summed = lax.psum(stacked, 'tensor')  128 us
    all_gather x1, blocking collectives, on_device(): every_query = lax.all_gather(grads[train_count:], 'dp', axis=0, tiled=True)  34.6 us
    dot_general x2, matrix products, partials(): jnp.dot(hidden.reshape(count, hidden.shape[2]), proj_in, preferred_elemen...  8.81 us
    dot_general x2, matrix products, partials(): jnp.dot(outgrad.reshape(count, outgrad.shape[2]), proj_out, preferred_ele...  5.35 us
  transfers between devices with their start and end apart: 1, of which 1 were waited for; matrix products, arithmetic and copies ran while one was open for 0% of the time, Pallas kernels for 0%

commit v1 on v0

v1 whole, which is shorter than its diff:
```python
import functools

import jax
import jax.numpy as jnp
from jax import lax
from jax.experimental import pallas as pl
from jax.experimental.pallas import tpu as pltpu
from jax.sharding import PartitionSpec as P

MESH = pl.DeviceIdType.MESH
HIGHEST = lax.Precision.HIGHEST
SEQS = 5
HALF = 512
OFFSETS = [
    (dx, dy, dc)
    for dx in (2, 1, 3, 0)
    for dy in (1, 0)
    for dc in (1, 0)
    if (dx, dy, dc) != (0, 0, 0)
]
PARTS = ((0, 320, "YX"), (320, 192, "XY"))
AFTER_CORE, AFTER_ONE, AFTER_TWO = 1, 4, 3
QUERY_STEP = 13


def kernel(
    ht, ot, hq, oq, pi, po, grads_ref, scores_ref,
    hb, ob, w, acc, cbuf, rbuf, mbuf, gsend, gbuf, qown, qbuf, sbuf,
    hbm_sem, core_ss, core_rs, ss, rs, g_ss, g_rs, q_ss, q_rs, s_ss, s_rs,
):
    t = lax.axis_index("tensor")
    group = lax.axis_index("dp")
    x, y, c = t // 4, (t // 2) % 2, t % 2

    def at(dx, dy, dc):
        xx = lax.rem(x + dx, 4)
        yy = 1 - y if dy else y
        cc = 1 - c if dc else c
        return {"tensor": (xx * 2 + yy) * 2 + cc}

    def row(v, m):
        return pl.multiple_of(v, m)

    loads = [
        pltpu.make_async_copy(pi, w.at[pl.ds(0, 64), pl.ds(0, 1792)], hbm_sem.at[0]),
        pltpu.make_async_copy(po, w.at[pl.ds(64, 64), pl.ds(1792, 512)], hbm_sem.at[1]),
    ]
    halves = [1 - c, c]
    for s in range(SEQS):
        for p in range(2):
            r = halves[p]
            i = 2 + (s * 2 + p) * 2
            h = hq.at[0, r] if s == 0 else ht.at[s - 1, r]
            o = oq.at[0, r] if s == 0 else ot.at[s - 1, r]
            here = pl.ds(p * HALF, HALF)
            loads.append(pltpu.make_async_copy(h, hb.at[s, here], hbm_sem.at[i]))
            loads.append(pltpu.make_async_copy(o, ob.at[s, here], hbm_sem.at[i + 1]))
    for load in loads:
        load.start()
    barrier = pltpu.get_barrier_semaphore()
    for off in OFFSETS:
        pl.semaphore_signal(barrier, inc=1, device_id=at(*off), device_id_type=MESH)
    for k in range(1, 8):
        pl.semaphore_signal(
            barrier, inc=1, device_id={"dp": lax.rem(group + k, 8)}, device_id_type=MESH
        )

    w[pl.ds(64, 64), pl.ds(0, 1792)] = jnp.zeros((64, 1792), jnp.bfloat16)
    w[pl.ds(0, 64), pl.ds(1792, 512)] = jnp.zeros((64, 512), jnp.bfloat16)
    loads[0].wait()
    loads[1].wait()

    def remote(src, dst, send, recv, device):
        return pltpu.make_async_remote_copy(
            src_ref=src, dst_ref=dst, send_sem=send, recv_sem=recv,
            device_id=device, device_id_type=MESH,
        )

    def compute(k):
        s, p = k // 2, k % 2
        r = pl.ds(row(p * HALF, HALF), HALF)
        i = 2 + k * 2
        pltpu.make_async_copy(hq.at[0, 0], hb.at[s, r], hbm_sem.at[i]).wait()
        pltpu.make_async_copy(oq.at[0, 0], ob.at[s, r], hbm_sem.at[i + 1]).wait()
        dims = (((1,), (1,)), ((), ()))
        total = lax.dot_general(
            hb[s, r], w[:, 0:1792], dims, preferred_element_type=jnp.float32
        )
        total = total + lax.dot_general(
            ob[s, r], w[:, 1792:2304], dims, preferred_element_type=jnp.float32
        )
        acc[s, r] = total

    def core_copy(s):
        return remote(
            acc.at[s, pl.ds(0, HALF)], cbuf.at[s], core_ss.at[s], core_rs.at[s], at(0, 0, 1)
        )

    def along(part, n):
        first, rows, way = part
        base = HALF + first
        if way == "YX":
            if n == 0:
                return "y", rows // 2, base, first
            return "x", rows // 8, base + y * (rows // 2), first + rows // 2
        if n == 0:
            return "x", rows // 4, base, first
        return "y", rows // 8, base + x * (rows // 4), first + 3 * (rows // 4)

    def copies(s, j, n):
        way, share, lo, off = along(PARTS[j], n)
        if way == "y":
            hops, sem = (0,), 0
        else:
            hops, sem = (2, 1, 3), 1
        found = []
        for k, dx in enumerate(hops):
            to = lax.rem(x + dx, 4) if way == "x" else 1 - y
            found.append(remote(
                acc.at[s, pl.ds(row(lo + to * share, 8), share)],
                rbuf.at[s, pl.ds(off + k * share, share)],
                ss.at[s, j, sem + k], rs.at[s, j, sem + k],
                at(dx, 0, 0) if way == "x" else at(0, 1, 0),
            ))
        return found

    def arrive(s, j, n):
        way, share, lo, off = along(PARTS[j], n)
        arrived = copies(s, j, n)
        for copy in arrived:
            copy.wait_recv()
        mine = pl.ds(row(lo + (x if way == "x" else y) * share, 8), share)
        total = acc[s, mine]
        for k in range(len(arrived)):
            total = total + rbuf[s, pl.ds(off + k * share, share)]
        return mine, total

    lane = lax.broadcasted_iota(jnp.int32, (16, 128), 1)

    def partial_grad(s):
        both = jnp.concatenate([arrive(s, j, 1)[1] for j in range(len(PARTS))], axis=0)
        wide = lax.broadcasted_iota(jnp.int32, both.shape, 1)
        twice = jnp.where(wide < 64, pltpu.roll(both, 64, 1), both)
        outer = lax.dot_general(
            both, twice, (((0,), (0,)), ((), ())), precision=HIGHEST,
            preferred_element_type=jnp.float32,
        )
        mbuf[...] = outer[0:64]
        for h in range(2):
            even = mbuf[pl.ds(2 * h, 16, stride=4)]
            odd = mbuf[pl.ds(2 * h + 1, 16, stride=4)]
            gsend[jnp.minimum(s, 1), h, pl.ds(s, 16, stride=8)] = jnp.where(lane < 64, even, odd)

    def spread(slot):
        found = []
        for k, off in enumerate(OFFSETS):
            to = at(*off)
            found.append(remote(
                gsend.at[slot, :, pl.ds(row(to["tensor"] * 8, 8), 8)], gbuf.at[slot, k],
                g_ss.at[slot, k], g_rs.at[slot, k], to,
            ))
        return found

    def collect(slot):
        for copy in spread(slot):
            copy.wait_recv()
        total = gsend[slot, :, pl.ds(row(t * 8, 8), 8)]
        for k in range(15):
            total = total + gbuf[slot, k]
        return total * (1.0 / 32.0)

    def query_copies():
        return [
            remote(
                qown, qbuf.at[group], q_ss.at[k - 1], q_rs.at[k - 1],
                {"dp": lax.rem(group + k, 8)},
            )
            for k in range(1, 8)
        ]

    def score_copies():
        return [
            remote(sbuf.at[t], sbuf.at[t], s_ss.at[k], s_rs.at[k], at(*off))
            for k, off in enumerate(OFFSETS)
        ]

    def when_due(k, lag, act):
        s2 = k - 1 - lag

        @pl.when((s2 >= 0) & (s2 % 2 == 0) & (s2 < 2 * SEQS))
        def _():
            act(s2 // 2)

    def after_core(s):
        core_copy(s).wait_recv()
        own = pl.ds(HALF, HALF)
        acc[s, own] = acc[s, own] + cbuf[s]
        for j in range(len(PARTS)):
            for copy in copies(s, j, 0):
                copy.start()

    def after_one(s):
        for j in range(len(PARTS)):
            mine, total = arrive(s, j, 0)
            acc[s, mine] = total
            for copy in copies(s, j, 1):
                copy.start()

    def after_two(s):
        partial_grad(s)

        @pl.when(s == 0)
        def _():
            for copy in spread(0):
                copy.start()

    gsend[...] = jnp.zeros_like(gsend)

    def half_step(k, carry):
        @pl.when(k < 2 * SEQS)
        def _():
            compute(k)

        @pl.when(k == 0)
        def _():
            pl.semaphore_wait(barrier, 22)

        @pl.when((k % 2 == 0) & (k < 2 * SEQS))
        def _():
            core_copy(k // 2).start()

        when_due(k, AFTER_CORE, after_core)
        when_due(k, AFTER_CORE + AFTER_ONE, after_one)
        when_due(k, AFTER_CORE + AFTER_ONE + AFTER_TWO, after_two)

        @pl.when(k == QUERY_STEP)
        def _():
            qown[...] = collect(0)
            qbuf[group] = qown[...]
            for copy in query_copies():
                copy.start()

        return carry

    lax.fori_loop(0, 2 * SEQS + AFTER_CORE + AFTER_ONE + AFTER_TWO, half_step, 0)

    for copy in spread(1):
        copy.start()
    grads = collect(1)
    for copy in query_copies():
        copy.wait_recv()
    part = jnp.zeros((8, 8), jnp.float32)
    for h in range(2):
        queries = jnp.concatenate([qbuf[k, h, 0:1] for k in range(8)], axis=0)
        part = part + lax.dot_general(
            grads[h], queries, (((1,), (1,)), ((), ())), precision=HIGHEST,
            preferred_element_type=jnp.float32,
        )
    sbuf[t, :, 0:8] = part
    for copy in score_copies():
        copy.start()
    for h in range(2):
        grads_ref[:, pl.ds(h * 128, 128)] = grads[h, 1:5]

    def sent(s, carry):
        core_copy(s).wait_send()
        for j in range(len(PARTS)):
            for n in range(2):
                for copy in copies(s, j, n):
                    copy.wait_send()
        return carry

    lax.fori_loop(0, SEQS, sent, 0)
    for copy in spread(0) + spread(1) + query_copies():
        copy.wait_send()
    for copy in score_copies():
        copy.wait_recv()
    total = sbuf[0]
    for k in range(1, 16):
        total = total + sbuf[k]
    scores_ref[...] = total[1:5, 0:8] * (1.0 / 64.0)
    for copy in score_copies():
        copy.wait_send()


def on_device(hidden_train, outgrad_train, hidden_query, outgrad_query, proj_in, proj_out):
    anywhere = pl.BlockSpec(memory_space=pl.ANY)
    vmem = pl.BlockSpec(memory_space=pltpu.VMEM)
    f32, bf16 = jnp.float32, jnp.bfloat16
    dma = pltpu.SemaphoreType.DMA
    return pl.pallas_call(
        kernel,
        out_shape=(jax.ShapeDtypeStruct((4, 256), f32), jax.ShapeDtypeStruct((4, 8), f32)),
        in_specs=[anywhere] * 6,
        out_specs=(vmem, vmem),
        scratch_shapes=[
            pltpu.VMEM((SEQS, 1024, 1792), bf16),
            pltpu.VMEM((SEQS, 1024, 512), bf16),
            pltpu.VMEM((128, 2304), bf16),
            pltpu.VMEM((SEQS, 1024, 128), f32),
            pltpu.VMEM((SEQS, HALF, 128), f32),
            pltpu.VMEM((SEQS, HALF, 128), f32),
            pltpu.VMEM((64, 128), f32),
            pltpu.VMEM((2, 2, 128, 128), f32),
            pltpu.VMEM((2, 15, 2, 8, 128), f32),
            pltpu.VMEM((2, 8, 128), f32),
            pltpu.VMEM((8, 2, 8, 128), f32),
            pltpu.VMEM((16, 8, 128), f32),
            dma((2 + SEQS * 4,)),
            dma((SEQS,)),
            dma((SEQS,)),
            dma((SEQS, 2, 4)),
            dma((SEQS, 2, 4)),
            dma((2, 15)),
            dma((2, 15)),
            dma((7,)),
            dma((7,)),
            dma((15,)),
            dma((15,)),
        ],
        compiler_params=pltpu.CompilerParams(
            collective_id=0, has_side_effects=True, vmem_limit_bytes=56 * 2**20
        ),
    )(
        *(
            a.reshape(a.shape[0], 2, HALF, a.shape[2])
            for a in (hidden_train, outgrad_train, hidden_query, outgrad_query)
        ),
        proj_in.T,
        proj_out.T,
    )


def solution(mesh):
    placed = (
        P("dp", None, "tensor"),
        P("dp", None, "tensor"),
        P("dp", None, "tensor"),
        P("dp", None, "tensor"),
        P("tensor", None),
        P("tensor", None),
    )
    return jax.shard_map(
        on_device,
        mesh=mesh,
        in_specs=placed,
        out_specs=(P("dp", "tensor"), P("dp", None)),
        check_vma=False,
    )
```

time: 205 us -> 42.6 us (0.21)
  the two profiles are of different devices: /device:TPU:0 before, /device:TPU:1 now
where the time goes in v1:
time: 42.6 us; the launch traced here: 42.4 us
  Pallas kernels  39.3 us (92%)
  local copies, waits for them, and re-layouts  2.5 us (6%)
  between operations  0.64 us (2%)
    pallas_call x1, Pallas kernels, on_device(): pl.pallas_call(kernel, out_shape=(jax.ShapeDtypeStruct((4, 256), f32), ja...  39.3 us
    unnamed x2, local copies, waits for them, and re-layouts  2.5 us

profile of v1, /device:TPU:1, one launch (start us, length us, event | category | flops | bytes accessed | tf_op | source)
XLA Modules:
  0.0 42.4 jit_solution(12455223137600495238)
XLA Ops:
  0.6 39.3 %shard_map.77 = (f32[4,256]{1,0:T(4,128)}, f32[4,8]{1,0:T(4,128)}) custom-call(bf16[4,2,512,1792]{3,2,1,0:T(8,128)(2,1)} %bitcast.6, bf16[4,2,512,512]{3,2,1,0:T(8,128)(2,1)} %bitcast.7, bf16[1,2,512,1792]{3,2,1,0:T(8,128)(2,1)} %bitcast.8, bf16[1,2,512,512]{3,2,1,0:T(8,128)(2,1)} %bitcast.9, bf16[64,1792]{1,0:T(8,128)(2,1)} %bitcast.10, ...), custom_call_target="tpu_custom_call" | custom-call | tf_op jit(solution)/shard_map/pallas_call | solution.py:291
  39.9 1.3 %copy.10 = f32[4,256]{1,0:T(4,128)} copy(f32[4,256]{1,0:T(4,128)} %get-tuple-element.4) | data formatting | bytes 8192
  41.2 1.2 %copy.11 = f32[4,8]{1,0:T(4,128)} copy(f32[4,8]{1,0:T(4,128)} %get-tuple-element.5) | data formatting | bytes 256

commit v2 on v1

v2 whole, which is shorter than its diff:
```python
import jax
import jax.numpy as jnp
from jax import lax
from jax.experimental import pallas as pl
from jax.experimental.pallas import tpu as pltpu
from jax.sharding import PartitionSpec as P

MESH = pl.DeviceIdType.MESH
HIGHEST = lax.Precision.HIGHEST
SEQS, CHUNKS, ROWS, HALF = 5, 10, 512, 256
OWN = HALF // 8
OFFSETS = [
    (dx, dy, dc)
    for dx in (2, 1, 3, 0)
    for dy in (1, 0)
    for dc in (1, 0)
    if (dx, dy, dc) != (0, 0, 0)
]
WAYS = ("YX", "XY")
TO_CORE, TO_ONE, TO_TWO = 1, 5, 9
QUERY_STEP = 15


def kernel(
    ht, ot, hq, oq, pi, po, out_ref,
    hb, ob, w, acc, cbuf, rbuf, fin, mbuf, gsend, gbuf, qbuf, sbuf,
    hbm_sem, core_ss, core_rs, ss, rs, g_ss, g_rs, q_ss, q_rs, s_ss, s_rs,
):
    t = lax.axis_index("tensor")
    group = lax.axis_index("dp")
    x, y, c = t // 4, (t // 2) % 2, t % 2

    def at(dx, dy, dc):
        xx = lax.rem(x + dx, 4)
        yy = 1 - y if dy else y
        cc = 1 - c if dc else c
        return {"tensor": (xx * 2 + yy) * 2 + cc}

    def row(v, m):
        return pl.multiple_of(v, m)

    loads = [
        pltpu.make_async_copy(pi, w.at[pl.ds(0, 64), pl.ds(0, 1792)], hbm_sem.at[0]),
        pltpu.make_async_copy(po, w.at[pl.ds(64, 64), pl.ds(1792, 512)], hbm_sem.at[1]),
    ]
    for k in range(CHUNKS):
        for p, side in enumerate((1 - c, c)):
            here = pl.ds(p * HALF, HALF)
            i = 2 + (k * 2 + p) * 2
            h = hq.at[0, k, side] if k < 2 else ht.at[k // 2 - 1, k % 2, side]
            o = oq.at[0, k, side] if k < 2 else ot.at[k // 2 - 1, k % 2, side]
            loads.append(pltpu.make_async_copy(h, hb.at[k, here], hbm_sem.at[i]))
            loads.append(pltpu.make_async_copy(o, ob.at[k, here], hbm_sem.at[i + 1]))
    for load in loads:
        load.start()
    barrier = pltpu.get_barrier_semaphore()
    for off in OFFSETS:
        pl.semaphore_signal(barrier, inc=1, device_id=at(*off), device_id_type=MESH)
    for k in range(1, 8):
        pl.semaphore_signal(
            barrier, inc=1, device_id={"dp": lax.rem(group + k, 8)}, device_id_type=MESH
        )
    w[pl.ds(64, 64), pl.ds(0, 1792)] = jnp.zeros((64, 1792), jnp.bfloat16)
    w[pl.ds(0, 64), pl.ds(1792, 512)] = jnp.zeros((64, 512), jnp.bfloat16)
    gsend[...] = jnp.zeros_like(gsend)
    loads[0].wait()
    loads[1].wait()

    def remote(src, dst, send, recv, device):
        return pltpu.make_async_remote_copy(
            src_ref=src, dst_ref=dst, send_sem=send, recv_sem=recv,
            device_id=device, device_id_type=MESH,
        )

    def compute(k):
        for p in range(2):
            i = 2 + (k * 2 + p) * 2
            here = pl.ds(p * HALF, HALF)
            pltpu.make_async_copy(hq.at[0, 0, 0], hb.at[k, here], hbm_sem.at[i]).wait()
            pltpu.make_async_copy(oq.at[0, 0, 0], ob.at[k, here], hbm_sem.at[i + 1]).wait()
        dims = (((1,), (1,)), ((), ()))
        total = lax.dot_general(
            hb[k], w[:, 0:1792], dims, preferred_element_type=jnp.float32
        )
        total = total + lax.dot_general(
            ob[k], w[:, 1792:2304], dims, preferred_element_type=jnp.float32
        )
        acc[k] = total

    def core_copy(k):
        return remote(
            acc.at[k, pl.ds(0, HALF)], cbuf.at[k], core_ss.at[k], core_rs.at[k], at(0, 0, 1)
        )

    def along(way, n):
        if way == "YX":
            if n == 0:
                return "y", HALF // 2, HALF, 0
            return "x", OWN, HALF + y * (HALF // 2), HALF // 2
        if n == 0:
            return "x", HALF // 4, HALF, 0
        return "y", OWN, HALF + x * (HALF // 4), 3 * (HALF // 4)

    def copies(k, way, n):
        axis, share, lo, off = along(way, n)
        if axis == "y":
            return [remote(
                acc.at[k, pl.ds(row(lo + (1 - y) * share, 8), share)],
                rbuf.at[k, pl.ds(off, share)], ss.at[k, 0], rs.at[k, 0], at(0, 1, 0),
            )]
        return [
            remote(
                acc.at[k, pl.ds(row(lo + lax.rem(x + dx, 4) * share, 8), share)],
                rbuf.at[k, pl.ds(off + q * share, share)],
                ss.at[k, 1 + q], rs.at[k, 1 + q], at(dx, 0, 0),
            )
            for q, dx in enumerate((2, 1, 3))
        ]

    def arrive(k, way, n):
        arrived = copies(k, way, n)
        for copy in arrived:
            copy.wait_recv()
        axis, share, lo, off = along(way, n)
        lo = lo + (x if axis == "x" else y) * share
        mine = pl.ds(row(lo, 8), share)
        total = acc[k, mine]
        for q in range(len(arrived)):
            total = total + rbuf[k, pl.ds(off + q * share, share)]
        return mine, total

    lane = lax.broadcasted_iota(jnp.int32, (16, 128), 1)

    def partial_grad(s):
        both = fin[pl.ds(row(s * 2 * OWN, 8), 2 * OWN)]
        wide = lax.broadcasted_iota(jnp.int32, both.shape, 1)
        twice = jnp.where(wide < 64, pltpu.roll(both, 64, 1), both)
        outer = lax.dot_general(
            both, twice, (((0,), (0,)), ((), ())), precision=HIGHEST,
            preferred_element_type=jnp.float32,
        )
        mbuf[...] = outer[0:64]
        for h in range(2):
            even = mbuf[pl.ds(2 * h, 16, stride=4)]
            odd = mbuf[pl.ds(2 * h + 1, 16, stride=4)]
            first = h * 4 + jnp.maximum(s - 1, 0)
            gsend[jnp.minimum(s, 1), pl.ds(first, 16, stride=8)] = jnp.where(lane < 64, even, odd)

    def spread(slot):
        found = []
        for q, off in enumerate(OFFSETS):
            to = at(*off)
            found.append(remote(
                gsend.at[slot, pl.ds(row(to["tensor"] * 8, 8), 8)], gbuf.at[slot, q],
                g_ss.at[slot, q], g_rs.at[slot, q], to,
            ))
        return found

    def collect(slot):
        for copy in spread(slot):
            copy.wait_recv()
        total = gsend[slot, pl.ds(row(t * 8, 8), 8)]
        for q in range(15):
            total = total + gbuf[slot, q]
        return total * (1.0 / 32.0)

    def query_copies():
        return [
            remote(
                qbuf.at[group], qbuf.at[group], q_ss.at[q - 1], q_rs.at[q - 1],
                {"dp": lax.rem(group + q, 8)},
            )
            for q in range(1, 8)
        ]

    def score_copies():
        return [
            remote(sbuf.at[t], sbuf.at[t], s_ss.at[q], s_rs.at[q], at(*off))
            for q, off in enumerate(OFFSETS)
        ]

    def when_chunk(k, act):
        for p, way in enumerate(WAYS):
            pl.when((k >= 0) & (k < CHUNKS) & (lax.rem(k, 2) == p))(lambda way=way: act(k, way))

    def start(found):
        for copy in found:
            copy.start()

    def sum_core(k):
        core_copy(k).wait_recv()
        own = pl.ds(HALF, HALF)
        acc[k, own] = acc[k, own] + cbuf[k]

    def first_sum(k, way):
        mine, total = arrive(k, way, 0)
        acc[k, mine] = total
        start(copies(k, way, 1))

    def last_sum(k, way):
        fin[pl.ds(row(k * OWN, 8), OWN)] = arrive(k, way, 1)[1]

    def grads_due(k):
        @pl.when((k >= 0) & (k < CHUNKS) & (lax.rem(k, 2) == 1))
        def _():
            partial_grad(k // 2)

        @pl.when(k == 1)
        def _():
            start(spread(0))

    def step(n, carry):
        @pl.when(n < CHUNKS)
        def _():
            compute(n)

        @pl.when(n == 0)
        def _():
            pl.semaphore_wait(barrier, 22)

        @pl.when(n < CHUNKS)
        def _():
            core_copy(n).start()

        k = n - TO_CORE

        @pl.when((k >= 0) & (k < CHUNKS))
        def _():
            sum_core(k)

        when_chunk(k, lambda k, way: start(copies(k, way, 0)))
        when_chunk(n - TO_ONE, first_sum)
        when_chunk(n - TO_TWO, last_sum)
        grads_due(n - TO_TWO)

        @pl.when(n == QUERY_STEP)
        def _():
            qbuf[group] = collect(0)
            start(query_copies())

        return carry

    lax.fori_loop(0, CHUNKS + TO_TWO, step, 0)

    start(spread(1))
    grads = collect(1)
    for copy in query_copies():
        copy.wait_recv()
    parts = []
    for h in range(2):
        queries = jnp.concatenate([qbuf[q, h * 4 : h * 4 + 1] for q in range(8)], axis=0)
        parts.append(lax.dot_general(
            grads, queries, (((1,), (1,)), ((), ())), precision=HIGHEST,
            preferred_element_type=jnp.float32,
        ))
    sbuf[t, 0:4, 0:8] = parts[0][0:4] + parts[1][4:8]
    start(score_copies())
    out_ref[0] = grads

    def sent(s, carry):
        for p, way in enumerate(WAYS):
            k = s * 2 + p
            core_copy(k).wait_send()
            for copy in copies(k, way, 0) + copies(k, way, 1):
                copy.wait_send()
        return carry

    lax.fori_loop(0, SEQS, sent, 0)
    for copy in spread(0) + spread(1) + query_copies():
        copy.wait_send()
    for copy in score_copies():
        copy.wait_recv()
    total = sbuf[0]
    for q in range(1, 16):
        total = total + sbuf[q]
    out_ref[1] = total * (1.0 / 64.0)
    for copy in score_copies():
        copy.wait_send()


def unpack(packed, grads_ref, scores_ref):
    for h in range(2):
        grads_ref[:, pl.ds(h * 128, 128)] = packed[0, h * 4 : h * 4 + 4]
    scores_ref[...] = packed[1, 0:4, 0:8]


def on_device(hidden_train, outgrad_train, hidden_query, outgrad_query, proj_in, proj_out):
    anywhere = pl.BlockSpec(memory_space=pl.ANY)
    vmem = pl.BlockSpec(memory_space=pltpu.VMEM)
    f32, bf16 = jnp.float32, jnp.bfloat16
    dma = pltpu.SemaphoreType.DMA
    packed = pl.pallas_call(
        kernel,
        out_shape=jax.ShapeDtypeStruct((2, 8, 128), f32),
        in_specs=[anywhere] * 6,
        out_specs=vmem,
        scratch_shapes=[
            pltpu.VMEM((CHUNKS, ROWS, 1792), bf16),
            pltpu.VMEM((CHUNKS, ROWS, 512), bf16),
            pltpu.VMEM((128, 2304), bf16),
            pltpu.VMEM((CHUNKS, ROWS, 128), f32),
            pltpu.VMEM((CHUNKS, HALF, 128), f32),
            pltpu.VMEM((CHUNKS, HALF, 128), f32),
            pltpu.VMEM((CHUNKS * OWN, 128), f32),
            pltpu.VMEM((64, 128), f32),
            pltpu.VMEM((2, 128, 128), f32),
            pltpu.VMEM((2, 15, 8, 128), f32),
            pltpu.VMEM((8, 8, 128), f32),
            pltpu.VMEM((16, 8, 128), f32),
            dma((2 + CHUNKS * 4,)),
            dma((CHUNKS,)),
            dma((CHUNKS,)),
            dma((CHUNKS, 8)),
            dma((CHUNKS, 8)),
            dma((2, 15)),
            dma((2, 15)),
            dma((7,)),
            dma((7,)),
            dma((15,)),
            dma((15,)),
        ],
        compiler_params=pltpu.CompilerParams(
            collective_id=0, has_side_effects=True, vmem_limit_bytes=56 * 2**20
        ),
    )(
        *(
            a.reshape(a.shape[0], 2, 2, HALF, a.shape[2])
            for a in (hidden_train, outgrad_train, hidden_query, outgrad_query)
        ),
        proj_in.T,
        proj_out.T,
    )
    return pl.pallas_call(
        unpack,
        out_shape=(jax.ShapeDtypeStruct((4, 256), f32), jax.ShapeDtypeStruct((4, 8), f32)),
        in_specs=[vmem],
        out_specs=(vmem, vmem),
    )(packed)


def solution(mesh):
    placed = (
        P("dp", None, "tensor"),
        P("dp", None, "tensor"),
        P("dp", None, "tensor"),
        P("dp", None, "tensor"),
        P("tensor", None),
        P("tensor", None),
    )
    return jax.shard_map(
        on_device,
        mesh=mesh,
        in_specs=placed,
        out_specs=(P("dp", "tensor"), P("dp", None)),
        check_vma=False,
    )
```

time: 42.6 us -> 39.8 us (0.934)
  local copies, waits for them, and re-layouts: 2.5 us -> 0 us
    unnamed x2 -> x0, local copies, waits for them, and re-layouts: 2.5 us -> none
    pallas_call x1 -> x2, Pallas kernels: 39.3 us -> 39 us  [the longest x1 37.7 us: on_device(): pl.pallas_call(kernel, out_shape=jax.ShapeDtypeStruct((2, 8, 128), f32),...]
where the time goes in v2:
time: 39.8 us; the launch traced here: 39.7 us
  Pallas kernels  39 us (98%)
  between operations  0.64 us (2%)
    pallas_call x1, Pallas kernels, on_device(): pl.pallas_call(kernel, out_shape=jax.ShapeDtypeStruct((2, 8, 128), f32),...  37.7 us
    pallas_call x1, Pallas kernels, on_device(): pl.pallas_call(unpack, out_shape=(jax.ShapeDtypeStruct((4, 256), f32), ja...  1.29 us

profile of v2, /device:TPU:1, one launch (start us, length us, event | category | flops | bytes accessed | tf_op | source)
XLA Modules:
  0.0 39.7 jit_solution(11919938074423916280)
XLA Ops:
  0.6 37.7 %shard_map.77.packed = f32[2,8,128]{2,1,0:T(8,128)} custom-call(bf16[4,2,2,256,1792]{4,3,2,1,0:T(8,128)(2,1)} %bitcast.6, bf16[4,2,2,256,512]{4,3,2,1,0:T(8,128)(2,1)} %bitcast.7, bf16[1,2,2,256,1792]{4,3,2,1,0:T(8,128)(2,1)} %bitcast.8, bf16[1,2,2,256,512]{4,3,2,1,0:T(8,128)(2,1)} %bitcast.9, bf16[64,1792]{1,0:T(8,128)(2,1)} %bitcast.10, ...), custom_call_target="tpu_custom_call" | custom-call | tf_op jit(solution)/shard_map/pallas_call | solution.py:292
  38.4 1.3 %shard_map.78 = (f32[4,256]{1,0:T(4,128)}, f32[4,8]{1,0:T(4,128)}) custom-call(f32[2,8,128]{2,1,0:T(8,128)} %shard_map.77.packed), custom_call_target="tpu_custom_call" | custom-call | tf_op jit(solution)/shard_map/pallas_call | solution.py:333

commit v3 on v2

--- a/solution.py
+++ b/solution.py
@@ -39,6 +39,13 @@
     def row(v, m):
         return pl.multiple_of(v, m)
 
+    barrier = pltpu.get_barrier_semaphore()
+    for k in range(1, 8):
+        pl.semaphore_signal(
+            barrier, inc=1, device_id={"dp": lax.rem(group + k, 8)}, device_id_type=MESH
+        )
+    for off in OFFSETS:
+        pl.semaphore_signal(barrier, inc=1, device_id=at(*off), device_id_type=MESH)
     loads = [
         pltpu.make_async_copy(pi, w.at[pl.ds(0, 64), pl.ds(0, 1792)], hbm_sem.at[0]),
         pltpu.make_async_copy(po, w.at[pl.ds(64, 64), pl.ds(1792, 512)], hbm_sem.at[1]),
@@ -53,13 +60,6 @@
             loads.append(pltpu.make_async_copy(o, ob.at[k, here], hbm_sem.at[i + 1]))
     for load in loads:
         load.start()
-    barrier = pltpu.get_barrier_semaphore()
-    for off in OFFSETS:
-        pl.semaphore_signal(barrier, inc=1, device_id=at(*off), device_id_type=MESH)
-    for k in range(1, 8):
-        pl.semaphore_signal(
-            barrier, inc=1, device_id={"dp": lax.rem(group + k, 8)}, device_id_type=MESH
-        )
     w[pl.ds(64, 64), pl.ds(0, 1792)] = jnp.zeros((64, 1792), jnp.bfloat16)
     w[pl.ds(0, 64), pl.ds(1792, 512)] = jnp.zeros((64, 512), jnp.bfloat16)
     gsend[...] = jnp.zeros_like(gsend)

time: 39.8 us -> 39.6 us (level)
  no operation moved by 1% of the time
where the time goes in v3:
time: 39.6 us; the launch traced here: 39.5 us
  Pallas kernels  38.8 us (98%)
  between operations  0.64 us (2%)
    pallas_call x1, Pallas kernels, on_device(): pl.pallas_call(kernel, out_shape=jax.ShapeDtypeStruct((2, 8, 128), f32),...  37.5 us
    pallas_call x1, Pallas kernels, on_device(): pl.pallas_call(unpack, out_shape=(jax.ShapeDtypeStruct((4, 256), f32), ja...  1.29 us

profile of v3, /device:TPU:1, one launch (start us, length us, event | category | flops | bytes accessed | tf_op | source)
XLA Modules:
  0.0 39.5 jit_solution(8815557557956768952)
XLA Ops:
  0.6 37.5 %shard_map.77.packed = f32[2,8,128]{2,1,0:T(8,128)} custom-call(bf16[4,2,2,256,1792]{4,3,2,1,0:T(8,128)(2,1)} %bitcast.6, bf16[4,2,2,256,512]{4,3,2,1,0:T(8,128)(2,1)} %bitcast.7, bf16[1,2,2,256,1792]{4,3,2,1,0:T(8,128)(2,1)} %bitcast.8, bf16[1,2,2,256,512]{4,3,2,1,0:T(8,128)(2,1)} %bitcast.9, bf16[64,1792]{1,0:T(8,128)(2,1)} %bitcast.10, ...), custom_call_target="tpu_custom_call" | custom-call | tf_op jit(solution)/shard_map/pallas_call | solution.py:292
  38.2 1.3 %shard_map.78 = (f32[4,256]{1,0:T(4,128)}, f32[4,8]{1,0:T(4,128)}) custom-call(f32[2,8,128]{2,1,0:T(8,128)} %shard_map.77.packed), custom_call_target="tpu_custom_call" | custom-call | tf_op jit(solution)/shard_map/pallas_call | solution.py:333
